TPU v7x, 512 devices: a whole 4x8x8 slice. The times are simulated.
512 devices in a mesh: rep: 16 (over x_hi, z), fsdp: 32 (over x_lo, y, core).
Axes of the slice: x: 4 (x_hi: 2, x_lo: 2; x = x_hi * 2 + x_lo), y: 8, z: 8, core: 2. Of those that a mesh axis runs over, the one named last changes fastest.
Arguments:
- inputs: bfloat16 [16, 4096, 4608], P('rep', 'fsdp'), may hold values from -60 to 60, as said below
- targets: bfloat16 [16, 4096, 1024], P('rep', 'fsdp'), may hold values from -6 to 6
- local_weights: float32 [16, 4608, 1024], P('rep', 'fsdp'), may hold values from -6 to 6
- global_weights: float32 [4608, 128], P('fsdp'), may hold values from -6 to 6
- momentum: float32 [4608, 128], P('fsdp'), may hold values from -3 to 3
- fragment: int32 [1], replicated, may hold values from 0 to 4095
Outputs:
- new_local: float32 [16, 4608, 1024], P('rep', 'fsdp')
- input_grad: bfloat16 [16, 4096, 4608], P('rep', 'fsdp')
- new_momentum: float32 [4608, 128], P('fsdp')
- new_global: float32 [4608, 128], P('fsdp')
Inputs may be any that keep to these rules, and one draw needn't show every extreme that they name: `inputs`: finite values.
All inputs are finite; a program needn't handle non-finite values.
Results may differ from a plain program's by a relative error of at most 0.0058.
Values may be sent and summed in bfloat16 or wider, within the bound.
A program may use at most 64 MiB of HBM per device.

v0:
```python
import math

import jax
import jax.numpy as jnp
from jax import lax
from jax.sharding import PartitionSpec as P

inner_rate = 0.2
outer_rate = 0.7
momentum_decay = 0.9
blend_keep = 0.5


def shards(inputs, targets, local_weights, global_weights, momentum, fragment):
    values = inputs[0].astype(jnp.float32)
    scale = lax.rsqrt(jnp.mean(values * values, axis=-1, keepdims=True) + 1e-06)
    unrounded = values * scale
    normed = unrounded.astype(jnp.bfloat16)
    owned = lax.all_to_all(normed, "fsdp", split_axis=1, concat_axis=0, tiled=True)
    weights_half = local_weights[0].astype(jnp.bfloat16)
    out_root = math.sqrt(targets.shape[2])
    piece = lax.all_gather(targets[0], "fsdp", axis=0, tiled=True)
    total = lax.dot_general(
        owned, piece, (((0,), (0,)), ((), ())), preferred_element_type=jnp.float32
    )
    d_piece = (
        lax.dot_general(
            piece, weights_half, (((1,), (1,)), ((), ())), preferred_element_type=jnp.float32
        )
        / out_root
    )
    d_owned = d_piece.astype(jnp.bfloat16)
    grad, d_owned = (total, d_owned)
    d_normed = lax.all_to_all(d_owned, "fsdp", split_axis=0, concat_axis=1, tiled=True).astype(
        jnp.float32
    )
    inner_prod = jnp.mean(d_normed * unrounded, axis=-1, keepdims=True)
    input_grad = (scale * (d_normed - unrounded * inner_prod)).astype(jnp.bfloat16)
    frag_width = global_weights.shape[1]
    frag_count = local_weights.shape[2] // frag_width
    start = fragment[0] % frag_count * frag_width
    frag_local = lax.dynamic_slice_in_dim(local_weights[0], start, frag_width, 1)
    delta = global_weights - frag_local
    replicas = lax.axis_size("rep")
    mean_delta = lax.psum(delta, "rep") / replicas
    new_momentum = momentum_decay * momentum + mean_delta
    new_global = global_weights - outer_rate * (mean_delta + momentum_decay * new_momentum)
    tokens_all = inputs.shape[1] * lax.axis_size("fsdp")
    inner = local_weights[0] - inner_rate * grad / math.sqrt(tokens_all)
    frag_inner = lax.dynamic_slice_in_dim(inner, start, frag_width, 1)
    blended = blend_keep * frag_inner + (1.0 - blend_keep) * new_global
    new_local = lax.dynamic_update_slice_in_dim(inner, blended, start, 1)
    return (new_local[None], input_grad[None], new_momentum, new_global)


def solution(mesh):
    placed = (
        P("rep", "fsdp", None),
        P("rep", "fsdp", None),
        P("rep", "fsdp", None),
        P("fsdp", None),
        P("fsdp", None),
        P(),
    )
    return jax.shard_map(
        shards,
        mesh=mesh,
        in_specs=placed,
        out_specs=(
            P("rep", "fsdp", None),
            P("rep", "fsdp", None),
            P("fsdp", None),
            P("fsdp", None),
        ),
        check_vma=False,
    )
```

profile of v0, /device:TPU:16, one launch (start us, length us, event | category | flops | bytes accessed | tf_op | source)
XLA Modules:
  0.0 306.0 jit_solution(16140192171722670136)
XLA Ops:
  8.0 0.0 all-gather.3.cloned.1.call-start
  8.0 0.7 all-gather.3.cloned.1.call-update
  8.7 81.3 %all-gather.3.cloned.1.call-done = bf16[1,4096,1024]{2,1,0:T(8,128)(2,1)} async-done(((bf16[1,128,1024]{2,1,0:T(8,128)(2,1)}), bf16[1,4096,1024]{2,1,0:T(8,128)(2,1)}) %all-gather.3.cloned.1.call-update) | async-done | bytes 8388624 | tf_op jit(solution)/shard_map/all_gather | solution.py:22
  90.0 6.4 %fusion.13 = bf16[18,32,8,128]{3,2,1,0:T(8,128)(2,1)S(1)} fusion(bf16[1,4096,1024]{2,1,0:T(8,128)(2,1)} %all-gather.3.cloned.1.call-done, f32[1,144,1024]{2,1,0:T(8,128)} %param.8), kind=kOutput, calls=%fused_computation.13 | convolution fusion | flops 1209139200 | bytes 10158080 | tf_op jit(solution)/shard_map/dot_general | solution.py:27
  96.3 0.0 copy-start
  96.4 1.2 copy.26
  97.6 6.9 %all-to-all-start.1 = ((bf16[32,128,144]{1,2,0:T(8,128)(2,1)}), bf16[32,128,144]{1,2,0:T(8,128)(2,1)S(1)}, u32[]{:S(2)}, u32[]{:S(2)}) async-start(bf16[32,128,144]{1,2,0:T(8,128)(2,1)} %bitcast.59), calls=%async_computation.1 | async-start | bytes 2359296 | tf_op jit(solution)/shard_map/all_to_all | solution.py:34
  104.4 0.0 copy-done
  104.4 0.7 copy.15
  105.2 0.6 multiply_reduce_fusion
  105.8 28.2 %all-to-all-done.1 = bf16[32,128,144]{1,2,0:T(8,128)(2,1)S(1)} async-done(((bf16[32,128,144]{1,2,0:T(8,128)(2,1)}), bf16[32,128,144]{1,2,0:T(8,128)(2,1)S(1)}, u32[]{:S(2)}, u32[]{:S(2)}) %all-to-all-start.1) | async-done | bytes 1179680 | tf_op jit(solution)/shard_map/all_to_all | solution.py:34
  134.0 0.7 fusion.12
  134.7 1.3 multiply_convert_fusion
  135.9 5.7 %all-to-all-start = ((bf16[128,32,144]{0,2,1:T(8,128)(2,1)}), bf16[128,32,144]{0,2,1:T(8,128)(2,1)S(1)}, u32[]{:S(2)}, u32[]{:S(2)}) async-start(bf16[128,32,144]{0,2,1:T(8,128)(2,1)} %multiply_convert_fusion), calls=%async_computation | async-start | bytes 2359296 | tf_op jit(solution)/shard_map/all_to_all | solution.py:19
  141.6 0.0 all-reduce.2.cloned.1.call-start
  142.4 1.6 bitcast_subtract_fusion.1
  143.9 0.0 all-reduce.2.cloned.1.call-update
  144.0 0.2 convert_element_type.60
  144.1 0.5 fusion.11
  144.6 0.0 copy-start.1
  144.6 1.4 copy.18
  146.0 0.0 copy-start.3
  146.0 0.0 copy-start.4
  146.0 25.2 %all-to-all-done = bf16[128,32,144]{0,2,1:T(8,128)(2,1)S(1)} async-done(((bf16[128,32,144]{0,2,1:T(8,128)(2,1)}), bf16[128,32,144]{0,2,1:T(8,128)(2,1)S(1)}, u32[]{:S(2)}, u32[]{:S(2)}) %all-to-all-start) | async-done | bytes 1179680 | tf_op jit(solution)/shard_map/all_to_all | solution.py:19
  171.2 0.0 copy-done.1
  171.2 4.8 %fusion.19 = f32[144,1024]{1,0:T(8,128)S(1)} fusion(bf16[1,4096,1024]{2,1,0:T(8,128)(2,1)} %all-gather.3.cloned.1.call-done, f32[1,144,1024]{2,1,0:T(8,128)S(1)} %copy-done.1, bf16[128,32,144]{0,2,1:T(8,128)(2,1)S(1)} %all-to-all-done), kind=kOutput, calls=%fused_computation.15 | convolution fusion | flops 1208254464 | bytes 10747904 | tf_op jit(solution)/shard_map/dot_general | solution.py:23
  176.0 120.1 %all-reduce.2.cloned.1.call-done = f32[144,128]{1,0:T(8,128)} async-done(((f32[144,128]{1,0:T(8,128)}), f32[144,128]{1,0:T(8,128)}) %all-reduce.2.cloned.1.call-update) | async-done | bytes 73744 | tf_op jit(solution)/shard_map/psum | solution.py:45
  296.2 0.0 copy-done.3
  296.2 0.0 copy-done.4
  296.2 1.6 bitcast_dynamic-update-slice_fusion
  297.7 0.0 copy-start.2
  297.7 0.8 copy-done.2
  (3 shorter events, 0.1 us)
Async XLA Ops:
  8.0 82.0 %all-gather.3.cloned.1.call-start = ((), (), s32[]{:S(2)}) async-start(), calls=%async_computation.3 | async-start | bytes 8650752 | tf_op jit(solution)/shard_map/all_gather | solution.py:22
  96.3 8.1 %copy-start = (bf16[1,128,4608]{2,1,0:T(8,128)(2,1)S(1)}, bf16[1,128,4608]{2,1,0:T(8,128)(2,1)}, u32[]{:S(2)}) copy-start(bf16[1,128,4608]{2,1,0:T(8,128)(2,1)} %param.6) | copy-start | bytes 3538948
  97.6 36.4 %all-to-all-start.1 = ((bf16[32,128,144]{1,2,0:T(8,128)(2,1)}), bf16[32,128,144]{1,2,0:T(8,128)(2,1)S(1)}, u32[]{:S(2)}, u32[]{:S(2)}) async-start(bf16[32,128,144]{1,2,0:T(8,128)(2,1)} %bitcast.59), calls=%async_computation.1 | async-start | bytes 2359296 | tf_op jit(solution)/shard_map/all_to_all | solution.py:34
  135.9 35.3 %all-to-all-start = ((bf16[128,32,144]{0,2,1:T(8,128)(2,1)}), bf16[128,32,144]{0,2,1:T(8,128)(2,1)S(1)}, u32[]{:S(2)}, u32[]{:S(2)}) async-start(bf16[128,32,144]{0,2,1:T(8,128)(2,1)} %multiply_convert_fusion), calls=%async_computation | async-start | bytes 2359296 | tf_op jit(solution)/shard_map/all_to_all | solution.py:19
  141.6 154.5 %all-reduce.2.cloned.1.call-start = ((), (), s32[]{:S(2)}) async-start(), calls=%async_computation.2 | async-start | bytes 147456 | tf_op jit(solution)/shard_map/psum | solution.py:45
  144.6 26.6 %copy-start.1 = (f32[1,144,1024]{2,1,0:T(8,128)S(1)}, f32[1,144,1024]{2,1,0:T(8,128)}, u32[]{:S(2)}) copy-start(f32[1,144,1024]{2,1,0:T(8,128)} %param.8) | copy-start | bytes 1769476
  146.0 150.2 %copy-start.3 = (f32[144,128]{1,0:T(8,128)S(1)}, f32[144,128]{1,0:T(8,128)}, u32[]{:S(2)}) copy-start(f32[144,128]{1,0:T(8,128)} %param.9) | copy-start | bytes 221188
  146.0 150.2 %copy-start.4 = (f32[144,128]{1,0:T(8,128)S(1)}, f32[144,128]{1,0:T(8,128)}, u32[]{:S(2)}) copy-start(f32[144,128]{1,0:T(8,128)} %param.10) | copy-start | bytes 221188
  297.7 0.8 copy-start.2
Sparse Core Ops, SparseCore 0:
  11.0 78.9 all-gather.2
Sparse Core Ops, SparseCore 1:
  145.6 150.5 all-reduce.1
where the time goes:
time: 307 us; the launch traced here: 306 us
  waiting for transfers between devices  255 us (83%)
  between operations  16.2 us (5%)
  starting transfers between devices  12.6 us (4%)
  matrix products  11.1 us (4%)
  other arithmetic  6.33 us (2%)
  local copies, waits for them, and re-layouts  4.23 us (1%)
    psum x1, waiting for transfers between devices, shards(): mean_delta = lax.psum(delta, 'rep') / replicas  120 us
    all_gather x1, waiting for transfers between devices, shards(): piece = lax.all_gather(targets[0], 'fsdp', axis=0, tiled=True)  81.3 us
    all_to_all x1, waiting for transfers between devices, shards(): lax.all_to_all(d_owned, 'fsdp', split_axis=0, concat_axis=1, tiled=True)  28.2 us
    all_to_all x1, waiting for transfers between devices, shards(): lax.all_to_all(normed, 'fsdp', split_axis=1, concat_axis=0, tiled=True)  25.2 us
    all_to_all x1, starting transfers between devices, shards(): lax.all_to_all(d_owned, 'fsdp', split_axis=0, concat_axis=1, tiled=True)  6.85 us
    dot_general x1, matrix products, shards(): lax.dot_general(piece, weights_half, (((1,), (1,)), ((), ())), preferred_...  6.35 us
  transfers between devices with their start and end apart: 4, of which 4 were waited for; matrix products, arithmetic and copies ran while one was open for 3% of the time, Pallas kernels for 0%

commit v1 on v0

v1 whole, which is shorter than its diff:
```python
import functools
import math

import jax
import jax.numpy as jnp
from jax import lax
from jax.experimental import pallas as pl
from jax.experimental.pallas import tpu as pltpu
from jax.sharding import PartitionSpec as P

MESH = pl.DeviceIdType.MESH
bf16 = jnp.bfloat16
f32 = jnp.float32

inner_rate = 0.2
outer_rate = 0.7
momentum_decay = 0.9
blend_keep = 0.5


def kernel(
    n_rep, n_y, tokens_all,
    frag_ref, x_ref, t_ref, lw_ref, gw_ref, mom_ref,
    nl_ref, ig_ref, nm_ref, ng_ref,
    wown, wg, tg, nown, nrm, nT, G, dout, din, rsA, rsB, rsout, gtot, gsend, scale_ref, racc, rin,
    w_snd, w_rcv, wp_snd, tg_snd, tg_rcv, n_snd, n_rcv, d_snd, d_rcv,
    rs_snd, rsA_rcv, rsB_rcv, tot_snd, tot_rcv, r_snd, r_rcv,
):
    rep = lax.axis_index("rep")
    me = lax.axis_index("fsdp")
    half = n_y // 2
    c = lax.rem(me, 2)
    y = lax.rem(me // 2, n_y)
    xl = me // (2 * n_y)
    a = xl * 2 + c
    rows, hidden = lw_ref.shape
    tok, width = x_ref.shape
    quarter = width // 4
    origin = y // half == c

    def dev(x_, y_, c_):
        return x_ * (2 * n_y) + y_ * 2 + c_

    up = dev(xl, lax.rem(y + 1, n_y), c)
    dn = dev(xl, lax.rem(y + n_y - 1, n_y), c)
    mate = dev(xl, y, 1 - c)
    across = dev(1 - xl, y, c)
    diag = dev(1 - xl, y, 1 - c)
    a_mate, a_across, a_diag = xl * 2 + 1 - c, (1 - xl) * 2 + c, (1 - xl) * 2 + 1 - c

    masks = []
    m = n_rep // 2
    while m:
        masks.append(m)
        m //= 2
    rep_peers = [rep + m * (1 - 2 * lax.rem(rep // m, 2)) for m in masks]

    def copy(src, dst, ss, rs, to, r=None):
        return pltpu.make_async_remote_copy(
            src_ref=src, dst_ref=dst, send_sem=ss, recv_sem=rs,
            device_id=(rep if r is None else r, to), device_id_type=MESH,
        )

    def blk(ref, j):
        return ref.at[pl.ds(pl.multiple_of(j * rows, 16), rows), :]

    def ds_blk(j):
        return pl.ds(pl.multiple_of(j * rows, 16), rows)

    def tok_ds(k, n=1):
        return pl.ds(pl.multiple_of(k * tok, 16), n * tok)

    barrier = pltpu.get_barrier_semaphore()
    for peer in (up, dn, mate, across, diag):
        pl.semaphore_signal(barrier, inc=1, device_id=(rep, peer), device_id_type=MESH)
    for peer in rep_peers:
        pl.semaphore_signal(barrier, inc=1, device_id=(peer, me), device_id_type=MESH)
    pl.semaphore_wait(barrier, 5 + len(rep_peers))

    def slot(o, f):
        return 2 * (o - half * c) + (c if f == 0 else 1 - c)

    wown[...] = lw_ref[...].astype(bf16)
    j0 = 2 * (y - half * c) + c
    j1 = 2 * (y - half * c) + 1 - c
    jm = 2 * (y - half * (1 - c)) + c

    @pl.when(origin)
    def _():
        copy(wown, blk(wg, j0), w_snd.at[0, j0], w_rcv.at[j0], up).start()
        copy(wown, blk(wg, j0), w_snd.at[1, j0], w_rcv.at[j0], dn).start()

    @pl.when(jnp.logical_not(origin))
    def _():
        copy(wown, blk(wg, jm), wp_snd, w_rcv.at[jm], mate).start()

    tg[tok_ds(a), :] = t_ref[...]

    def tblk(k):
        return tg.at[tok_ds(k), :]

    copy(tblk(a), tblk(a), tg_snd.at[0], tg_rcv.at[a], across).start()
    copy(tblk(a), tblk(a), tg_snd.at[1], tg_rcv.at[a], mate).start()

    @pl.when(origin)
    def _():
        wg[ds_blk(j0), :] = wown[...]

    step = 16

    def norm_rows(i, _):
        r = pl.ds(pl.multiple_of(i * step, step), step)
        v = x_ref[r, :].astype(f32)
        sc = lax.rsqrt(jnp.sum(v * v, axis=-1, keepdims=True) * (1.0 / width) + 1e-06)
        scale_ref[r, :] = sc
        nv = (v * sc).astype(bf16)
        for k in range(4):
            nown[k, r, :] = nv[:, k * quarter : (k + 1) * quarter]
        return 0

    lax.fori_loop(0, tok // step, norm_rows, 0)

    def nblk(k):
        return nrm.at[tok_ds(k), :]

    n_copies = [
        copy(nown.at[k], nblk(a), n_snd.at[k], n_rcv.at[a], to)
        for k, to in ((a_across, across), (a_diag, diag), (a_mate, mate))
    ]
    for cp in n_copies:
        cp.start()
    nrm[tok_ds(a), :] = nown[a]

    picked = jnp.full((rows, 128), lax.rem(frag_ref[0], hidden // 128), jnp.int32)
    frag_local = lw_ref[:, :128]
    for k in range(1, hidden // 128):
        frag_local = jnp.where(picked == k, lw_ref[:, k * 128 : (k + 1) * 128], frag_local)
    racc[0] = gw_ref[...] - frag_local

    def r_copy(i):
        return copy(racc.at[i], rin.at[i], r_snd.at[i], r_rcv.at[i], me, rep_peers[i])

    r_copy(0).start()

    def rep_step(i):
        if i < len(masks):
            r_copy(i).wait_recv()
            racc[i + 1] = racc[i] + rin[i]
            if i + 1 < len(masks):
                r_copy(i + 1).start()

    @pl.when(origin)
    def _():
        first = copy(blk(wg, j1), blk(wg, j1), w_snd.at[0, j1], w_rcv.at[j1], up)
        first.wait_recv()
        first.start()
        copy(blk(wg, j1), blk(wg, j1), w_snd.at[1, j1], w_rcv.at[j1], dn).start()

    def ways(f):
        return ((1, half - f, up, 0), (-1, half - 1 + f, dn, 1))

    def gather_step(s):
        for f in (0, 1):
            for sign, hops, to, d in ways(f):
                if s > hops:
                    continue
                o = lax.rem(y - sign * s + n_y, n_y)

                @pl.when(o // half == c)
                def _():
                    j = slot(o, f)
                    cp = copy(blk(wg, j), blk(wg, j), w_snd.at[d, j], w_rcv.at[j], to)
                    cp.wait_recv()
                    if s + 1 <= hops:
                        cp.start()

    gather_step(1)
    relay = copy(tblk(a_across), tblk(a_across), tg_snd.at[2], tg_rcv.at[a_across], mate)
    relay.wait_recv()
    relay.start()
    rep_step(0)
    gather_step(2)
    rep_step(1)
    gather_step(3)
    rep_step(2)

    for k, to in ((a_mate, mate), (a_diag, mate)):
        copy(tblk(k), tblk(k), tg_snd.at[1], tg_rcv.at[k], to).wait_recv()
    for k, to in ((a_mate, mate), (a_across, across), (a_diag, diag)):
        copy(nown.at[k], nblk(k), n_snd.at[k], n_rcv.at[k], to).wait_recv()
    mt = quarter // 3 if quarter % 384 == 0 else quarter
    nt = 256
    for i in range(quarter // mt):
        nT[i * mt : (i + 1) * mt, :] = nrm[:, i * mt : (i + 1) * mt].T
    for i in range(quarter // mt):
        for n in range(hidden // nt):
            G[i * mt : (i + 1) * mt, n * nt : (n + 1) * nt] = jnp.dot(
                nT[i * mt : (i + 1) * mt, :], tg[:, n * nt : (n + 1) * nt], preferred_element_type=f32
            )

    def rs_ways(f):
        return ((1, half - f, dn, rsA, rsA_rcv), (-1, half - 1 + f, up, rsB, rsB_rcv))

    def reduce_step(s):
        for f in (1, 0):
            for sign, hops, to, buf, sem in rs_ways(f):
                if s > hops:
                    continue
                o = lax.rem(y - sign * s + n_y, n_y)

                @pl.when(o // half == c)
                def _():
                    j = slot(o, f)
                    cp = copy(blk(rsout, j), blk(buf, j), rs_snd.at[j], sem.at[j], to)
                    if s < hops:
                        cp.wait_recv()
                        rsout[ds_blk(j), :] = (G[ds_blk(j), :] + buf[ds_blk(j), :].astype(f32)).astype(bf16)
                    else:
                        rsout[ds_blk(j), :] = G[ds_blk(j), :].astype(bf16)
                    cp.start()

    reduce_step(4)
    gather_step(4)
    rep_step(3)

    def d_part(base):
        r = tok_ds(base, 2)
        for i in range(quarter // mt):
            v = lax.dot_general(
                tg[r, :], wg[i * mt : (i + 1) * mt, :], (((1,), (1,)), ((), ())), preferred_element_type=f32
            )
            dout[r, i * mt : (i + 1) * mt] = (v * (1.0 / math.sqrt(hidden))).astype(bf16)

    def d_copy(k, to):
        return copy(dout.at[tok_ds(k), :], din.at[a], d_snd.at[k], d_rcv.at[a], to)

    d_part((1 - xl) * 2)
    d_copy(a_across, across).start()
    d_copy(a_diag, diag).start()
    reduce_step(3)
    d_part(xl * 2)
    d_copy(a_mate, mate).start()
    din[a] = dout[tok_ds(a), :]
    reduce_step(2)
    reduce_step(1)

    for k, to in ((a_mate, mate), (a_across, across), (a_diag, diag)):
        copy(dout.at[tok_ds(a), :], din.at[k], d_snd.at[k], d_rcv.at[k], to).wait_recv()

    def grad_rows(i, _):
        r = pl.ds(pl.multiple_of(i * step, step), step)
        sc = scale_ref[r, :]
        total = jnp.zeros((step, 1), f32)
        for k in range(4):
            u = x_ref[r, k * quarter : (k + 1) * quarter].astype(f32) * sc
            total += jnp.sum(din[k, r, :].astype(f32) * u, axis=-1, keepdims=True)
        mean = total * (1.0 / width)
        for k in range(4):
            u = x_ref[r, k * quarter : (k + 1) * quarter].astype(f32) * sc
            ig_ref[r, k * quarter : (k + 1) * quarter] = (sc * (din[k, r, :].astype(f32) - u * mean)).astype(bf16)
        return 0

    lax.fori_loop(0, tok // step, grad_rows, 0)

    mean_delta = racc[len(masks)] / n_rep
    new_m = momentum_decay * mom_ref[...] + mean_delta
    new_g = gw_ref[...] - outer_rate * (mean_delta + momentum_decay * new_m)
    nm_ref[...] = new_m
    ng_ref[...] = new_g

    def tot_copy():
        return copy(gsend, gtot, tot_snd, tot_rcv, mate)

    @pl.when(origin)
    def _():
        for j, out in ((j1, gsend), (j0, gtot)):
            copy(blk(rsout, j), blk(rsA, j), rs_snd.at[j], rsA_rcv.at[j], dn).wait_recv()
            copy(blk(rsout, j), blk(rsB, j), rs_snd.at[j], rsB_rcv.at[j], up).wait_recv()
            r = ds_blk(j)
            out[...] = G[r, :] + rsA[r, :].astype(f32) + rsB[r, :].astype(f32)
            if out is gsend:
                tot_copy().start()
        tot_copy().wait_send()

    @pl.when(jnp.logical_not(origin))
    def _():
        tot_copy().wait_recv()

    for k in range(hidden // 128):
        cols = slice(k * 128, (k + 1) * 128)
        inner = lw_ref[:, cols] - (inner_rate * gtot[:, cols]) * (1.0 / math.sqrt(tokens_all))
        blended = blend_keep * inner + (1.0 - blend_keep) * new_g
        nl_ref[:, cols] = jnp.where(picked == k, blended, inner)

    @pl.when(origin)
    def _():
        for j in (j0, j1):
            for d, to in ((0, up), (1, dn)):
                copy(blk(wg, j), blk(wg, j), w_snd.at[d, j], w_rcv.at[j], to).wait_send()

    @pl.when(jnp.logical_not(origin))
    def _():
        copy(wown, blk(wg, jm), wp_snd, w_rcv.at[jm], mate).wait_send()

    for s in range(1, half + 1):
        for f in (0, 1):
            for sign, hops, to, d in ways(f):
                o = lax.rem(y - sign * s + n_y, n_y)
                if s <= hops:

                    @pl.when(o // half == c)
                    def _():
                        j = slot(o, f)
                        if s + 1 <= hops:
                            copy(blk(wg, j), blk(wg, j), w_snd.at[d, j], w_rcv.at[j], to).wait_send()
                        copy(blk(rsout, j), blk(rsA, j), rs_snd.at[j], rsA_rcv.at[j], dn).wait_send()

    for i in range(3):
        copy(tblk(a), tblk(a), tg_snd.at[i], tg_rcv.at[a], mate).wait_send()
    for cp in n_copies:
        cp.wait_send()
    for k, to in ((a_across, across), (a_diag, diag), (a_mate, mate)):
        d_copy(k, to).wait_send()
    for i in range(len(masks)):
        r_copy(i).wait_send()


def solution(mesh):
    n_rep, n_fsdp = mesh.shape["rep"], mesh.shape["fsdp"]
    n_y = n_fsdp // 4

    def shards(inputs, targets, local_weights, global_weights, momentum, fragment):
        x, t, lw = inputs[0], targets[0], local_weights[0]
        tok, width = x.shape
        rows, hidden = lw.shape
        quarter = width // 4
        n_masks = max(n_rep.bit_length() - 1, 1)
        vmem = pl.BlockSpec(memory_space=pltpu.VMEM)
        dma = pltpu.SemaphoreType.DMA
        V = pltpu.VMEM
        outs = pl.pallas_call(
            functools.partial(kernel, n_rep, n_y, tok * n_fsdp),
            out_shape=(
                jax.ShapeDtypeStruct((rows, hidden), f32),
                jax.ShapeDtypeStruct((tok, width), bf16),
                jax.ShapeDtypeStruct(global_weights.shape, f32),
                jax.ShapeDtypeStruct(global_weights.shape, f32),
            ),
            in_specs=[pl.BlockSpec(memory_space=pltpu.SMEM)] + [vmem] * 5,
            out_specs=(vmem,) * 4,
            scratch_shapes=[
                V((rows, hidden), bf16),
                V((quarter, hidden), bf16),
                V((4 * tok, hidden), bf16),
                V((4, tok, quarter), bf16),
                V((4 * tok, quarter), bf16),
                V((quarter, 4 * tok), bf16),
                V((quarter, hidden), f32),
                V((4 * tok, quarter), bf16),
                V((4, tok, quarter), bf16),
                V((quarter, hidden), bf16),
                V((quarter, hidden), bf16),
                V((quarter, hidden), bf16),
                V((rows, hidden), f32),
                V((rows, hidden), f32),
                V((tok, 1), f32),
                V((n_masks + 1,) + global_weights.shape, f32),
                V((n_masks,) + global_weights.shape, f32),
                dma((2, 8)), dma((8,)), dma(()),
                dma((3,)), dma((4,)),
                dma((4,)), dma((4,)),
                dma((4,)), dma((4,)),
                dma((8,)), dma((8,)), dma((8,)),
                dma(()), dma(()),
                dma((n_masks,)), dma((n_masks,)),
            ],
            compiler_params=pltpu.CompilerParams(
                collective_id=0, has_side_effects=True, vmem_limit_bytes=48 * 1024 * 1024
            ),
        )(fragment, x, t, lw, global_weights, momentum)
        new_local, input_grad, new_m, new_g = outs
        return new_local[None], input_grad[None], new_m, new_g

    placed = (
        P("rep", "fsdp", None),
        P("rep", "fsdp", None),
        P("rep", "fsdp", None),
        P("fsdp", None),
        P("fsdp", None),
        P(),
    )
    return jax.shard_map(
        shards,
        mesh=mesh,
        in_specs=placed,
        out_specs=(
            P("rep", "fsdp", None),
            P("rep", "fsdp", None),
            P("fsdp", None),
            P("fsdp", None),
        ),
        check_vma=False,
    )
```

time: 307 us -> 95.7 us (0.31)
  the two profiles are of different devices: /device:TPU:16 before, /device:TPU:4 now
where the time goes in v1:
time: 95.7 us; the launch traced here: 95.3 us
  Pallas kernels  85.9 us (90%)
  local copies, waits for them, and re-layouts  8.14 us (9%)
  between operations  1.3 us (1%)
    pallas_call x1, Pallas kernels, shards(): pl.pallas_call(functools.partial(kernel, n_rep, n_y, tok * n_fsdp), out_s...  85.9 us
    unnamed x14, local copies, waits for them, and re-layouts  8.14 us

profile of v1, /device:TPU:4, one launch (start us, length us, event | category | flops | bytes accessed | tf_op | source)
XLA Modules:
  0.0 95.3 jit_solution(11766085509203861723)
XLA Ops:
  1.3 0.0 copy-start
  1.3 1.3 %copy-done = bf16[1,128,4608]{2,1,0:T(8,128)(2,1)S(1)} copy-done((bf16[1,128,4608]{2,1,0:T(8,128)(2,1)S(1)}, bf16[1,128,4608]{2,1,0:T(8,128)(2,1)}, u32[]{:S(2)}) %copy-start) | copy-done | bytes 1179672
  2.6 0.0 copy-start.1
  2.6 1.1 %copy-done.1 = f32[1,144,1024]{2,1,0:T(8,128)S(1)} copy-done((f32[1,144,1024]{2,1,0:T(8,128)S(1)}, f32[1,144,1024]{2,1,0:T(8,128)}, u32[]{:S(2)}) %copy-start.1) | copy-done | bytes 589848
  3.6 0.0 copy-start.2
  3.6 0.9 copy-done.2
  4.6 0.0 copy-start.3
  4.6 0.9 copy-done.3
  5.5 0.0 copy-start.4
  5.5 0.9 copy-done.4
  6.3 85.9 %shard_map.93 = (f32[144,1024]{1,0:T(8,128)S(1)}, bf16[128,4608]{1,0:T(8,128)(2,1)S(1)}, f32[144,128]{1,0:T(8,128)S(1)}, f32[144,128]{1,0:T(8,128)S(1)}) custom-call(s32[1]{0:T(128)S(6)} %copy.14.frag_ref, bf16[128,4608]{1,0:T(8,128)(2,1)S(1)} %bitcast.5, bf16[128,1024]{1,0:T(8,128)(2,1)S(1)} %bitcast.9, f32[144,1024]{1,0:T(8,128)S(1)} %bitcast.7, ...), custom_call_target="tpu_custom_call" | custom-call | tf_op jit(solution)/shard_map/pallas_call | solution.py:341
  92.3 0.8 copy.15
  93.1 1.0 %copy.16 = bf16[1,128,4608]{2,1,0:T(8,128)(2,1)} copy(bf16[1,128,4608]{2,1,0:T(8,128)(2,1)S(1)} %bitcast.6) | data formatting | bytes 2359296
  94.1 0.6 copy.17
  94.7 0.6 copy.18
Async XLA Ops:
  1.3 1.3 %copy-start = (bf16[1,128,4608]{2,1,0:T(8,128)(2,1)S(1)}, bf16[1,128,4608]{2,1,0:T(8,128)(2,1)}, u32[]{:S(2)}) copy-start(bf16[1,128,4608]{2,1,0:T(8,128)(2,1)} %param.6) | copy-start | bytes 3538948
  2.6 1.1 %copy-start.1 = (f32[1,144,1024]{2,1,0:T(8,128)S(1)}, f32[1,144,1024]{2,1,0:T(8,128)}, u32[]{:S(2)}) copy-start(f32[1,144,1024]{2,1,0:T(8,128)} %param.8) | copy-start | bytes 1769476
  3.6 0.9 copy-start.2
  4.6 0.9 copy-start.3
  5.5 0.9 copy-start.4

commit v2 on v0

v2 whole, which is shorter than its diff:
```python
import functools
import math

import jax
import jax.numpy as jnp
from jax import lax
from jax.experimental import pallas as pl
from jax.experimental.pallas import tpu as pltpu
from jax.sharding import PartitionSpec as P

MESH = pl.DeviceIdType.MESH
bf16 = jnp.bfloat16
f32 = jnp.float32

inner_rate = 0.2
outer_rate = 0.7
momentum_decay = 0.9
blend_keep = 0.5


def kernel(
    n_rep, n_y, tokens_all,
    frag_ref, x_hbm, t_hbm, lw_hbm, gw_hbm, mom_hbm,
    nl_out, ig_out, nm_out, ng_out,
    nl_ref, ig_ref, nm_ref, ng_ref, x_ref, lw_ref, gw_ref, mom_ref, wg, tg, xT, nown, nT, G, dout, din, rsA, rsB, rsout, igT, racc, rin,
    in_sem, out_sem, w_snd, w_rcv, tg_snd, tg_rcv, n_snd, n_rcv, d_snd, d_rcv, rs_snd, rsA_rcv, rsB_rcv, r_snd, r_rcv,
):
    rep = lax.axis_index("rep")
    me = lax.axis_index("fsdp")
    half = n_y // 2
    c = lax.rem(me, 2)
    y = lax.rem(me // 2, n_y)
    xl = me // (2 * n_y)
    a = xl * 2 + c
    rows, hidden = lw_ref.shape
    tok, width = x_ref.shape
    cut = (rows // 16 + 1) // 2 * 16
    parts = ((0, cut), (cut, rows - cut))

    def dev(x_, y_, c_):
        return x_ * (2 * n_y) + y_ * 2 + c_

    def wrap(v):
        return lax.rem(v + n_y, n_y)

    up = dev(xl, wrap(y + 1), c)
    dn = dev(xl, wrap(y - 1), c)
    mate = dev(xl, y, 1 - c)
    across = dev(1 - xl, y, c)
    diag = dev(1 - xl, y, 1 - c)
    a_mate, a_across, a_diag = xl * 2 + 1 - c, (1 - xl) * 2 + c, (1 - xl) * 2 + 1 - c

    masks = []
    m = 1
    while m < n_rep:
        masks.append(m)
        m *= 2
    rep_peers = [rep + m * (1 - 2 * lax.rem(rep // m, 2)) for m in masks]

    def copy(src, dst, ss, rs, to, r=None):
        return pltpu.make_async_remote_copy(
            src_ref=src, dst_ref=dst, send_sem=ss, recv_sem=rs,
            device_id=(rep if r is None else r, to), device_id_type=MESH,
        )

    def rows_of(j, f=None):
        first, n = (0, rows) if f is None else parts[f]
        return pl.ds(pl.multiple_of(j * rows + first, 16), n)

    loads = [
        pltpu.make_async_copy(src, dst, in_sem.at[i])
        for i, (src, dst) in enumerate(
            ((lw_hbm, lw_ref), (t_hbm, tg.at[a]), (x_hbm, x_ref), (gw_hbm, gw_ref), (mom_hbm, mom_ref))
        )
    ]
    for ld in loads:
        ld.start()

    barrier = pltpu.get_barrier_semaphore()
    for peer in (up, dn, mate, across, diag):
        pl.semaphore_signal(barrier, inc=1, device_id=(rep, peer), device_id_type=MESH)
    for peer in rep_peers:
        pl.semaphore_signal(barrier, inc=1, device_id=(peer, me), device_id_type=MESH)

    loads[0].wait()
    wg[rows_of(y), :] = lw_ref[...].astype(bf16)
    pl.semaphore_wait(barrier, 5 + len(rep_peers))

    flows = ((1, 0, half, up, 0), (-1, 1, half, dn, 1), (1, 1, half - 1, up, 0), (-1, 0, half - 1, dn, 1))

    def w_copy(o, f, to, d):
        blk = wg.at[rows_of(o, f), :]
        return copy(blk, blk, w_snd.at[d, o, f], w_rcv.at[o, f], to)

    for _, f, _, to, d in flows:
        w_copy(y, f, to, d).start()

    def gather_step(s):
        for sign, f, hops, to, d in flows:
            if s <= hops:
                cp = w_copy(wrap(y - sign * s), f, to, d)
                cp.wait_recv()
                if s + 1 <= hops:
                    cp.start()

    def t_copy(k, i, to):
        return copy(tg.at[k], tg.at[k], tg_snd.at[i], tg_rcv.at[k], to)

    loads[1].wait()
    t_copy(a, 0, across).start()
    t_copy(a, 1, mate).start()

    loads[2].wait()
    tile = 128
    total = jnp.zeros((1, tok), f32)
    for i in range(width // tile):
        v = x_ref[:, i * tile : (i + 1) * tile].T
        xT[i * tile : (i + 1) * tile, :] = v
        v = v.astype(f32)
        total += jnp.sum(v * v, axis=0, keepdims=True)
    scale = lax.rsqrt(total * (1.0 / width) + 1e-06)
    n_blocks = width // rows

    def place(p):
        return 2 * (p // (2 * n_y)) + p % 2, p // 2 % n_y

    for p in range(n_blocks):
        k, j = place(p)
        u = xT[p * rows : (p + 1) * rows, :].astype(f32) * scale
        nown[k, j * rows : (j + 1) * rows, :] = u.astype(bf16)

    plane = ((a_across, across), (a_diag, diag), (a_mate, mate))

    def n_copy(k, to):
        return copy(nown.at[k], nT.at[a], n_snd.at[k], n_rcv.at[a], to)

    for k, to in plane:
        n_copy(k, to).start()
    nT[a] = nown[a]

    loads[3].wait()
    loads[4].wait()
    picked = jnp.full((rows, 128), lax.rem(frag_ref[0], hidden // 128), jnp.int32)
    frag_local = lw_ref[:, :128]
    for k in range(1, hidden // 128):
        frag_local = jnp.where(picked == k, lw_ref[:, k * 128 : (k + 1) * 128], frag_local)
    racc[0] = gw_ref[...] - frag_local

    def r_copy(i):
        return copy(racc.at[i], rin.at[i], r_snd.at[i], r_rcv.at[i], me, rep_peers[i])

    r_copy(0).start()

    def rep_step(i):
        if i < len(masks):
            r_copy(i).wait_recv()
            racc[i + 1] = racc[i] + rin[i]
            if i + 1 < len(masks):
                r_copy(i + 1).start()

    def d_block(j):
        r = rows_of(j)
        v = lax.dot_general(
            wg[r, :], tg[...].reshape(4 * tok, hidden), (((1,), (1,)), ((), ())), preferred_element_type=f32
        )
        v = (v * (1.0 / math.sqrt(hidden))).astype(bf16)
        for k in range(4):
            dout[k, r, :] = v[:, k * tok : (k + 1) * tok]

    def g_block(j):
        r = rows_of(j)
        lhs = jnp.concatenate([nT[k, r, :] for k in range(4)], axis=1)
        wide = hidden // 2
        for n in range(2):
            cols = slice(n * wide, (n + 1) * wide)
            G[r, cols] = jnp.dot(lhs, tg[:, :, cols].reshape(4 * tok, wide), preferred_element_type=f32)

    def rs_copy(o, f, sign):
        buf, sem, to = (rsA, rsA_rcv, dn) if sign == 1 else (rsB, rsB_rcv, up)
        r = rows_of(o, f)
        return copy(rsout.at[r, :], buf.at[r, :], rs_snd.at[o, f], sem.at[o, f], to)

    def reduce_part(s, sign, f):
        hops = half if (sign == 1) == (f == 0) else half - 1
        o = wrap(y - sign * s)
        r = rows_of(o, f)
        cp = rs_copy(o, f, sign)
        if s < hops:
            cp.wait_recv()
            buf = rsA if sign == 1 else rsB
            rsout[r, :] = (G[r, :] + buf[r, :].astype(f32)).astype(bf16)
        else:
            rsout[r, :] = G[r, :].astype(bf16)
        cp.start()

    gather_step(1)
    relay = t_copy(a_across, 2, mate)
    relay.wait_recv()
    relay.start()
    gather_step(2)
    rep_step(0)
    for k in (a_mate, a_diag):
        t_copy(k, 1, mate).wait_recv()
    near = [wrap(y + s) for s in (0, 1, -1, 2, -2)]
    for j in near:
        d_block(j)
    gather_step(3)
    rep_step(1)
    for k, to in ((a_mate, mate), (a_across, across), (a_diag, diag)):
        copy(nown.at[k], nT.at[k], n_snd.at[k], n_rcv.at[k], to).wait_recv()
    far = wrap(y + half)
    g_block(far)
    reduce_part(4, 1, 0)
    reduce_part(4, -1, 1)
    for sign, f in ((1, 1), (-1, 0)):
        g_block(wrap(y - sign * 3))
        reduce_part(3, sign, f)
    d_block(wrap(y + 3))
    d_block(wrap(y - 3))
    gather_step(4)
    d_block(far)

    def d_copy(k, to):
        return copy(dout.at[k], din.at[a], d_snd.at[k], d_rcv.at[a], to)

    for k, to in plane:
        d_copy(k, to).start()
    din[a] = dout[a]
    rep_step(2)
    for s in (-2, 2, -1, 1, 0):
        g_block(wrap(y + s))
    for sign, f in ((1, 0), (-1, 1)):
        reduce_part(3, sign, f)
    for s in (2, 1):
        for sign, f in ((1, 1), (-1, 0), (1, 0), (-1, 1)):
            reduce_part(s, sign, f)
        if s == 2:
            rep_step(3)

    for k, to in ((a_mate, mate), (a_across, across), (a_diag, diag)):
        copy(dout.at[k], din.at[k], d_snd.at[k], d_rcv.at[k], to).wait_recv()
    total = jnp.zeros((1, tok), f32)
    for p in range(n_blocks):
        k, j = place(p)
        u = xT[p * rows : (p + 1) * rows, :].astype(f32) * scale
        d = din[k, j * rows : (j + 1) * rows, :].astype(f32)
        total += jnp.sum(d * u, axis=0, keepdims=True)
    mean = total * (1.0 / width)
    for p in range(n_blocks):
        k, j = place(p)
        u = xT[p * rows : (p + 1) * rows, :].astype(f32) * scale
        d = din[k, j * rows : (j + 1) * rows, :].astype(f32)
        igT[p * rows : (p + 1) * rows, :] = (scale * (d - u * mean)).astype(bf16)
    for i in range(width // tile):
        ig_ref[:, i * tile : (i + 1) * tile] = igT[i * tile : (i + 1) * tile, :].T

    outs = ((ig_ref, ig_out), (nm_ref, nm_out), (ng_ref, ng_out), (nl_ref, nl_out))
    stores = [pltpu.make_async_copy(src, dst, out_sem.at[i]) for i, (src, dst) in enumerate(outs)]
    stores[0].start()

    mean_delta = racc[len(masks)] / n_rep
    new_m = momentum_decay * mom_ref[...] + mean_delta
    nm_ref[...] = new_m
    ng_ref[...] = gw_ref[...] - outer_rate * (mean_delta + momentum_decay * new_m)
    stores[1].start()
    stores[2].start()

    for f in (1, 0):
        r = rows_of(y, f)
        own = slice(parts[f][0], sum(parts[f]))
        for sign in (1, -1):
            rs_copy(y, f, sign).wait_recv()
        for k in range(hidden // 128):
            cols = slice(k * 128, (k + 1) * 128)
            grad = G[r, cols] + rsA[r, cols].astype(f32) + rsB[r, cols].astype(f32)
            inner = lw_ref[own, cols] - (inner_rate * grad) * (1.0 / math.sqrt(tokens_all))
            blended = blend_keep * inner + (1.0 - blend_keep) * ng_ref[own, :]
            nl_ref[own, cols] = jnp.where(picked[own] == k, blended, inner)

    stores[3].start()

    for s in range(half):
        for sign, f, hops, to, d in flows:
            if s + 1 <= hops:
                w_copy(wrap(y - sign * s), f, to, d).wait_send()
    for s in range(1, n_y):
        for f in (0, 1):
            rs_copy(wrap(y + s), f, 1).wait_send()
    for i in range(3):
        t_copy(a, i, mate).wait_send()
    for k, to in plane:
        n_copy(k, to).wait_send()
        d_copy(k, to).wait_send()
    for i in range(len(masks)):
        r_copy(i).wait_send()
    for st in stores:
        st.wait()


def finish(nl_in, ig_in, nm_in, ng_in, nl_out, ig_out, nm_out, ng_out, nl_ref, ig_ref, nm_ref, ng_ref, in_sem, out_sem):
    def moves(pairs, sem):
        return [pltpu.make_async_copy(src, dst, sem.at[i]) for i, (src, dst) in enumerate(pairs)]

    held = (ig_ref, nl_ref, nm_ref, ng_ref)
    loads = moves(zip((ig_in, nl_in, nm_in, ng_in), held), in_sem)
    stores = moves(zip(held, (ig_out, nl_out, nm_out, ng_out)), out_sem)
    for ld in loads:
        ld.start()
    for ld, st in zip(loads, stores):
        ld.wait()
        st.start()
    for st in stores:
        st.wait()


def solution(mesh):
    n_rep, n_fsdp = mesh.shape["rep"], mesh.shape["fsdp"]
    n_y = n_fsdp // 4

    def shards(inputs, targets, local_weights, global_weights, momentum, fragment):
        x, t, lw = inputs[0], targets[0], local_weights[0]
        tok, width = x.shape
        rows, hidden = lw.shape
        quarter = width // 4
        small = global_weights.shape
        n_masks = max(n_rep.bit_length() - 1, 1)
        limit = 63 * 1024 * 1024
        smem = pl.BlockSpec(memory_space=pltpu.SMEM)
        hbm = pl.BlockSpec(memory_space=pltpu.HBM)
        dma = pltpu.SemaphoreType.DMA
        V = pltpu.VMEM
        shape = jax.ShapeDtypeStruct
        outs = pl.pallas_call(
            functools.partial(kernel, n_rep, n_y, tok * n_fsdp),
            out_shape=(shape((rows, hidden), f32), shape((tok, width), bf16), shape(small, f32), shape(small, f32)),
            in_specs=[smem] + [hbm] * 5,
            out_specs=(hbm,) * 4,
            scratch_shapes=[
                V((rows, hidden), f32),
                V((tok, width), bf16),
                V(small, f32),
                V(small, f32),
                V((tok, width), bf16),
                V((rows, hidden), f32),
                V(small, f32),
                V(small, f32),
                V((quarter, hidden), bf16),
                V((4, tok, hidden), bf16),
                V((width, tok), bf16),
                V((4, quarter, tok), bf16),
                V((4, quarter, tok), bf16),
                V((quarter, hidden), f32),
                V((4, quarter, tok), bf16),
                V((4, quarter, tok), bf16),
                V((quarter, hidden), bf16),
                V((quarter, hidden), bf16),
                V((quarter, hidden), bf16),
                V((width, tok), bf16),
                V((n_masks + 1,) + small, f32),
                V((n_masks,) + small, f32),
                dma((5,)), dma((4,)),
                dma((2, n_y, 2)), dma((n_y, 2)),
                dma((3,)), dma((4,)),
                dma((4,)), dma((4,)),
                dma((4,)), dma((4,)),
                dma((n_y, 2)), dma((n_y, 2)), dma((n_y, 2)),
                dma((n_masks,)), dma((n_masks,)),
            ],
            compiler_params=pltpu.CompilerParams(
                collective_id=0, has_side_effects=True, vmem_limit_bytes=limit
            ),
        )(fragment, x, t, lw, global_weights, momentum)
        new_local, input_grad, new_m, new_g = pl.pallas_call(
            finish,
            out_shape=(shape((rows, hidden), f32), shape((tok, width), bf16), shape(small, f32), shape(small, f32)),
            in_specs=[hbm] * 4,
            out_specs=(hbm,) * 4,
            scratch_shapes=[
                V((rows, hidden), f32), V((tok, width), bf16), V(small, f32), V(small, f32), dma((4,)), dma((4,))
            ],
            compiler_params=pltpu.CompilerParams(vmem_limit_bytes=limit),
        )(*outs)
        return new_local[None], input_grad[None], new_m, new_g

    placed = (
        P("rep", "fsdp", None),
        P("rep", "fsdp", None),
        P("rep", "fsdp", None),
        P("fsdp", None),
        P("fsdp", None),
        P(),
    )
    return jax.shard_map(
        shards,
        mesh=mesh,
        in_specs=placed,
        out_specs=(
            P("rep", "fsdp", None),
            P("rep", "fsdp", None),
            P("fsdp", None),
            P("fsdp", None),
        ),
        check_vma=False,
    )
```

time: 307 us -> 65 us (0.21)
  the two profiles are of different devices: /device:TPU:16 before, /device:TPU:2 now
where the time goes in v2:
time: 65 us; the launch traced here: 64.8 us
  Pallas kernels  63.5 us (98%)
  between operations  1.29 us (2%)
    pallas_call x1, Pallas kernels, shards(): pl.pallas_call(functools.partial(kernel, n_rep, n_y, tok * n_fsdp), out_s...  60.9 us
    pallas_call x1, Pallas kernels, shards(): pl.pallas_call(finish, out_shape=(shape((rows, hidden), f32), shape((tok,...  2.58 us

profile of v2, /device:TPU:2, one launch (start us, length us, event | category | flops | bytes accessed | tf_op | source)
XLA Modules:
  0.0 64.8 jit_solution(1404098150456268569)
XLA Ops:
  1.3 60.9 %shard_map.93 = (f32[144,1024]{1,0:T(8,128)}, bf16[128,4608]{1,0:T(8,128)(2,1)}, f32[144,128]{1,0:T(8,128)}, f32[144,128]{1,0:T(8,128)}) custom-call(s32[1]{0:T(128)S(6)} %copy.10.frag_ref, bf16[128,4608]{1,0:T(8,128)(2,1)} %bitcast.5, bf16[128,1024]{1,0:T(8,128)(2,1)} %bitcast.7, f32[144,1024]{1,0:T(8,128)} %bitcast.6, f32[144,128]{1,0:T(8,128)} %gw_hbm.1, ...), custom_call_target="tpu_custom_call" | custom-call | tf_op jit(solution)/shard_map/pallas_call | solution.py:333
  62.2 2.6 %shard_map.94 = (f32[144,1024]{1,0:T(8,128)}, bf16[128,4608]{1,0:T(8,128)(2,1)}, f32[144,128]{1,0:T(8,128)}, f32[144,128]{1,0:T(8,128)}) custom-call(f32[144,1024]{1,0:T(8,128)} %get-tuple-element.12.nl_in, bf16[128,4608]{1,0:T(8,128)(2,1)} %get-tuple-element.13.ig_in, f32[144,128]{1,0:T(8,128)} %get-tuple-element.14.nm_in, f32[144,128]{1,0:T(8,128)} %get-tuple-element.15.ng_in), custom_call_target="tpu_custom_call" | custom-call | tf_op jit(solution)/shard_map/pallas_call | solution.py:373

commit v3 on v2

--- a/solution.py
+++ b/solution.py
@@ -22,8 +22,9 @@
     n_rep, n_y, tokens_all,
     frag_ref, x_hbm, t_hbm, lw_hbm, gw_hbm, mom_hbm,
     nl_out, ig_out, nm_out, ng_out,
-    nl_ref, ig_ref, nm_ref, ng_ref, x_ref, lw_ref, gw_ref, mom_ref, wg, tg, xT, nown, nT, G, dout, din, rsA, rsB, rsout, igT, racc, rin,
-    in_sem, out_sem, w_snd, w_rcv, tg_snd, tg_rcv, n_snd, n_rcv, d_snd, d_rcv, rs_snd, rsA_rcv, rsB_rcv, r_snd, r_rcv,
+    nl_ref, ig_ref, nm_ref, ng_ref, x_ref, lw_ref, gw_ref, mom_ref, wg, tg, xT, nown, nT, G, dout, din, rsA, rsB, rsout, igT, delta, rsum, ed, zin, pair, full,
+    in_sem, out_sem, w_snd, w_rcv, tg_snd, tg_rcv, n_snd, n_rcv, d_snd, d_rcv, rs_snd, rsA_rcv, rsB_rcv,
+    go, e_snd, e_rcv, b_snd, b_rcv, z_snd, z_rcv, p_snd, p_rcv, f_snd, f_rcv,
 ):
     rep = lax.axis_index("rep")
     me = lax.axis_index("fsdp")
@@ -50,12 +51,13 @@
     diag = dev(1 - xl, y, 1 - c)
     a_mate, a_across, a_diag = xl * 2 + 1 - c, (1 - xl) * 2 + c, (1 - xl) * 2 + 1 - c
 
-    masks = []
-    m = 1
-    while m < n_rep:
-        masks.append(m)
-        m *= 2
-    rep_peers = [rep + m * (1 - 2 * lax.rem(rep // m, 2)) for m in masks]
+    n_z = n_rep // 2
+    z = lax.rem(rep, n_z)
+    x_peer = (1 - rep // n_z) * n_z + z
+
+    def z_peer(t):
+        zt = lax.rem(z + t, n_z)
+        return zt, rep // n_z * n_z + zt
 
     def copy(src, dst, ss, rs, to, r=None):
         return pltpu.make_async_remote_copy(
@@ -76,15 +78,48 @@
     for ld in loads:
         ld.start()
 
+    is_guide = a == 1
+    is_summer = a == 3
+    guide = dev(0, y, 1)
+    summer = dev(1, y, 1)
     barrier = pltpu.get_barrier_semaphore()
-    for peer in (up, dn, mate, across, diag):
-        pl.semaphore_signal(barrier, inc=1, device_id=(rep, peer), device_id_type=MESH)
-    for peer in rep_peers:
-        pl.semaphore_signal(barrier, inc=1, device_id=(peer, me), device_id_type=MESH)
+
+    def tell(sem, to, r=None):
+        pl.semaphore_signal(sem, inc=1, device_id=(rep if r is None else r, to), device_id_type=MESH)
+
+    @pl.when(a != 3)
+    def _():
+        tell(barrier, up)
+        tell(barrier, dn)
+
+    @pl.when(a != 1)
+    def _():
+        tell(barrier, guide)
+
+    @pl.when(is_summer)
+    def _():
+        tell(barrier, dev(0, wrap(y + 1), 1))
+        tell(barrier, dev(0, wrap(y - 1), 1))
+        tell(barrier, me, x_peer)
+        for t in range(1, n_z):
+            tell(barrier, me, z_peer(t)[1])
 
     loads[0].wait()
     wg[rows_of(y), :] = lw_ref[...].astype(bf16)
-    pl.semaphore_wait(barrier, 5 + len(rep_peers))
+
+    @pl.when(c == 0)
+    def _():
+        pl.semaphore_wait(barrier, 2)
+
+    @pl.when(is_guide)
+    def _():
+        pl.semaphore_wait(barrier, 7)
+        for to in (dev(1, y, 1), dev(0, y, 0), dev(1, y, 0)):
+            tell(go, to)
+
+    @pl.when(is_summer)
+    def _():
+        pl.semaphore_wait(go, 1)
 
     flows = ((1, 0, half, up, 0), (-1, 1, half, dn, 1), (1, 1, half - 1, up, 0), (-1, 0, half - 1, dn, 1))
 
@@ -106,9 +141,12 @@
     def t_copy(k, i, to):
         return copy(tg.at[k], tg.at[k], tg_snd.at[i], tg_rcv.at[k], to)
 
+    def t_send():
+        t_copy(a, 0, across).start()
+        t_copy(a, 1, mate).start()
+
     loads[1].wait()
-    t_copy(a, 0, across).start()
-    t_copy(a, 1, mate).start()
+    pl.when(c == 1)(t_send)
 
     loads[2].wait()
     tile = 128
@@ -134,29 +172,91 @@
     def n_copy(k, to):
         return copy(nown.at[k], nT.at[a], n_snd.at[k], n_rcv.at[a], to)
 
-    for k, to in plane:
-        n_copy(k, to).start()
-    nT[a] = nown[a]
-
     loads[3].wait()
     loads[4].wait()
     picked = jnp.full((rows, 128), lax.rem(frag_ref[0], hidden // 128), jnp.int32)
     frag_local = lw_ref[:, :128]
     for k in range(1, hidden // 128):
         frag_local = jnp.where(picked == k, lw_ref[:, k * 128 : (k + 1) * 128], frag_local)
-    racc[0] = gw_ref[...] - frag_local
-
-    def r_copy(i):
-        return copy(racc.at[i], rin.at[i], r_snd.at[i], r_rcv.at[i], me, rep_peers[i])
-
-    r_copy(0).start()
-
-    def rep_step(i):
-        if i < len(masks):
-            r_copy(i).wait_recv()
-            racc[i + 1] = racc[i] + rin[i]
-            if i + 1 < len(masks):
-                r_copy(i + 1).start()
+    delta[...] = gw_ref[...] - frag_local
+
+    def e_copy(k):
+        return copy(delta, ed.at[pl.ds(pl.multiple_of(k * rows, 8), rows), :], e_snd, e_rcv.at[k], summer)
+
+    def b_copy(k, to):
+        return copy(full.at[pl.ds(pl.multiple_of(k * rows, 8), rows), :], rsum, b_snd.at[k], b_rcv, to)
+
+    @pl.when(c == 0)
+    def _():
+        pl.semaphore_wait(go, 1)
+        t_send()
+
+    @pl.when(a != 3)
+    def _():
+        e_copy(a).start()
+
+    for k, to in plane:
+        n_copy(k, to).start()
+    nT[a] = nown[a]
+
+    piece = 4 * rows // n_z
+    others = ((0, dev(0, y, 0)), (1, dev(0, y, 1)), (2, dev(1, y, 0)))
+
+    def piece_of(zt):
+        return pl.ds(pl.multiple_of(zt * piece, 8), piece)
+
+    def z_copy(t):
+        zt, peer = z_peer(t)
+        return copy(ed.at[piece_of(zt), :], zin.at[z], z_snd.at[t], z_rcv.at[z], me, peer)
+
+    def f_copy(t):
+        blk = full.at[piece_of(z), :]
+        return copy(blk, blk, f_snd.at[t], f_rcv.at[z], me, z_peer(t)[1])
+
+    def p_copy():
+        return copy(pair.at[0], pair.at[1], p_snd, p_rcv, me, x_peer)
+
+    def rep_start():
+        @pl.when(is_summer)
+        def _():
+            ed[3 * rows :, :] = delta[...]
+            for k, to in others:
+                e_copy(k).wait_recv()
+            pl.semaphore_wait(barrier, n_z)
+            for t in range(1, n_z):
+                z_copy(t).start()
+            zin[z] = ed[piece_of(z), :]
+
+    def rep_over_z():
+        @pl.when(is_summer)
+        def _():
+            for t in range(1, n_z):
+                zt, peer = z_peer(t)
+                copy(zin.at[zt], zin.at[zt], z_snd.at[t], z_rcv.at[zt], me, peer).wait_recv()
+            total = zin[0]
+            for zt in range(1, n_z):
+                total = total + zin[zt]
+            pair[0] = total
+            p_copy().start()
+
+    def rep_over_x():
+        @pl.when(is_summer)
+        def _():
+            p_copy().wait_recv()
+            full[piece_of(z), :] = pair[0] + pair[1]
+            for t in range(1, n_z):
+                f_copy(t).start()
+
+    def rep_end():
+        @pl.when(is_summer)
+        def _():
+            for t in range(1, n_z):
+                zt, peer = z_peer(t)
+                blk = full.at[piece_of(zt), :]
+                copy(blk, blk, f_snd.at[t], f_rcv.at[zt], me, peer).wait_recv()
+            for k, to in others:
+                b_copy(k, to).start()
+            rsum[...] = full[3 * rows :, :]
 
     def d_block(j):
         r = rows_of(j)
@@ -197,15 +297,15 @@
     relay = t_copy(a_across, 2, mate)
     relay.wait_recv()
     relay.start()
+    rep_start()
     gather_step(2)
-    rep_step(0)
     for k in (a_mate, a_diag):
         t_copy(k, 1, mate).wait_recv()
     near = [wrap(y + s) for s in (0, 1, -1, 2, -2)]
     for j in near:
         d_block(j)
     gather_step(3)
-    rep_step(1)
+    rep_over_z()
     for k, to in ((a_mate, mate), (a_across, across), (a_diag, diag)):
         copy(nown.at[k], nT.at[k], n_snd.at[k], n_rcv.at[k], to).wait_recv()
     far = wrap(y + half)
@@ -225,8 +325,8 @@
 
     for k, to in plane:
         d_copy(k, to).start()
+    rep_over_x()
     din[a] = dout[a]
-    rep_step(2)
     for s in (-2, 2, -1, 1, 0):
         g_block(wrap(y + s))
     for sign, f in ((1, 0), (-1, 1)):
@@ -235,7 +335,7 @@
         for sign, f in ((1, 1), (-1, 0), (1, 0), (-1, 1)):
             reduce_part(s, sign, f)
         if s == 2:
-            rep_step(3)
+            rep_end()
 
     for k, to in ((a_mate, mate), (a_across, across), (a_diag, diag)):
         copy(dout.at[k], din.at[k], d_snd.at[k], d_rcv.at[k], to).wait_recv()
@@ -258,7 +358,11 @@
     stores = [pltpu.make_async_copy(src, dst, out_sem.at[i]) for i, (src, dst) in enumerate(outs)]
     stores[0].start()
 
-    mean_delta = racc[len(masks)] / n_rep
+    @pl.when(a != 3)
+    def _():
+        b_copy(a, summer).wait_recv()
+
+    mean_delta = rsum[...] / n_rep
     new_m = momentum_decay * mom_ref[...] + mean_delta
     nm_ref[...] = new_m
     ng_ref[...] = gw_ref[...] - outer_rate * (mean_delta + momentum_decay * new_m)
@@ -291,8 +395,19 @@
     for k, to in plane:
         n_copy(k, to).wait_send()
         d_copy(k, to).wait_send()
-    for i in range(len(masks)):
-        r_copy(i).wait_send()
+    @pl.when(a != 3)
+    def _():
+        e_copy(a).wait_send()
+
+    @pl.when(is_summer)
+    def _():
+        p_copy().wait_send()
+        for t in range(1, n_z):
+            z_copy(t).wait_send()
+            f_copy(t).wait_send()
+        for k, to in others:
+            b_copy(k, to).wait_send()
+
     for st in stores:
         st.wait()
 
@@ -323,7 +438,7 @@
         rows, hidden = lw.shape
         quarter = width // 4
         small = global_weights.shape
-        n_masks = max(n_rep.bit_length() - 1, 1)
+        n_z = n_rep // 2
         limit = 63 * 1024 * 1024
         smem = pl.BlockSpec(memory_space=pltpu.SMEM)
         hbm = pl.BlockSpec(memory_space=pltpu.HBM)
@@ -356,15 +471,21 @@
                 V((quarter, hidden), bf16),
                 V((quarter, hidden), bf16),
                 V((width, tok), bf16),
-                V((n_masks + 1,) + small, f32),
-                V((n_masks,) + small, f32),
+                V(small, f32),
+                V(small, f32),
+                V((4 * rows, small[1]), f32),
+                V((n_z, 4 * rows // n_z, small[1]), f32),
+                V((2, 4 * rows // n_z, small[1]), f32),
+                V((4 * rows, small[1]), f32),
                 dma((5,)), dma((4,)),
                 dma((2, n_y, 2)), dma((n_y, 2)),
                 dma((3,)), dma((4,)),
                 dma((4,)), dma((4,)),
                 dma((4,)), dma((4,)),
                 dma((n_y, 2)), dma((n_y, 2)), dma((n_y, 2)),
-                dma((n_masks,)), dma((n_masks,)),
+                pltpu.SemaphoreType.REGULAR,
+                dma(()), dma((4,)), dma((4,)), dma(()),
+                dma((n_z,)), dma((n_z,)), dma(()), dma(()), dma((n_z,)), dma((n_z,)),
             ],
             compiler_params=pltpu.CompilerParams(
                 collective_id=0, has_side_effects=True, vmem_limit_bytes=limit

time: 65 us -> 58.9 us (0.906)
  the two profiles are of different devices: /device:TPU:2 before, /device:TPU:1 now
where the time goes in v3:
time: 58.9 us; the launch traced here: 58.7 us
  Pallas kernels  57.4 us (97%)
  between operations  1.29 us (2%)
    pallas_call x1, Pallas kernels, shards(): pl.pallas_call(functools.partial(kernel, n_rep, n_y, tok * n_fsdp), out_s...  54.9 us
    pallas_call x1, Pallas kernels, shards(): pl.pallas_call(finish, out_shape=(shape((rows, hidden), f32), shape((tok,...  2.58 us

profile of v3, /device:TPU:1, one launch (start us, length us, event | category | flops | bytes accessed | tf_op | source)
XLA Modules:
  0.0 58.7 jit_solution(58719116483393817)
XLA Ops:
  1.3 54.9 %shard_map.93 = (f32[144,1024]{1,0:T(8,128)}, bf16[128,4608]{1,0:T(8,128)(2,1)}, f32[144,128]{1,0:T(8,128)}, f32[144,128]{1,0:T(8,128)}) custom-call(s32[1]{0:T(128)S(6)} %copy.10.frag_ref, bf16[128,4608]{1,0:T(8,128)(2,1)} %bitcast.5, bf16[128,1024]{1,0:T(8,128)(2,1)} %bitcast.7, f32[144,1024]{1,0:T(8,128)} %bitcast.6, f32[144,128]{1,0:T(8,128)} %gw_hbm.1, ...), custom_call_target="tpu_custom_call" | custom-call | tf_op jit(solution)/shard_map/pallas_call | solution.py:448
  56.1 2.6 %shard_map.94 = (f32[144,1024]{1,0:T(8,128)}, bf16[128,4608]{1,0:T(8,128)(2,1)}, f32[144,128]{1,0:T(8,128)}, f32[144,128]{1,0:T(8,128)}) custom-call(f32[144,1024]{1,0:T(8,128)} %get-tuple-element.12.nl_in, bf16[128,4608]{1,0:T(8,128)(2,1)} %get-tuple-element.13.ig_in, f32[144,128]{1,0:T(8,128)} %get-tuple-element.14.nm_in, f32[144,128]{1,0:T(8,128)} %get-tuple-element.15.ng_in), custom_call_target="tpu_custom_call" | custom-call | tf_op jit(solution)/shard_map/pallas_call | solution.py:494

commit v4 on v3

--- a/solution.py
+++ b/solution.py
@@ -19,7 +19,7 @@
 
 
 def kernel(
-    n_rep, n_y, tokens_all,
+    n_rep, n_y, tokens_all, n_parts,
     frag_ref, x_hbm, t_hbm, lw_hbm, gw_hbm, mom_hbm,
     nl_out, ig_out, nm_out, ng_out,
     nl_ref, ig_ref, nm_ref, ng_ref, x_ref, lw_ref, gw_ref, mom_ref, wg, tg, xT, nown, nT, G, dout, din, rsA, rsB, rsout, igT, delta, rsum, ed, zin, pair, full,
@@ -35,8 +35,11 @@
     a = xl * 2 + c
     rows, hidden = lw_ref.shape
     tok, width = x_ref.shape
-    cut = (rows // 16 + 1) // 2 * 16
-    parts = ((0, cut), (cut, rows - cut))
+    units, parts, first = rows // 16, [], 0
+    for f in range(n_parts):
+        n = 16 * (units // n_parts + (f < units % n_parts))
+        parts.append((first, n, 1 - 2 * (f % 2)))
+        first += n
 
     def dev(x_, y_, c_):
         return x_ * (2 * n_y) + y_ * 2 + c_
@@ -44,8 +47,9 @@
     def wrap(v):
         return lax.rem(v + n_y, n_y)
 
-    up = dev(xl, wrap(y + 1), c)
-    dn = dev(xl, wrap(y - 1), c)
+    turn = 1 - 2 * c
+    up = dev(xl, wrap(y + turn), c)
+    dn = dev(xl, wrap(y - turn), c)
     mate = dev(xl, y, 1 - c)
     across = dev(1 - xl, y, c)
     diag = dev(1 - xl, y, 1 - c)
@@ -66,16 +70,18 @@
         )
 
     def rows_of(j, f=None):
-        first, n = (0, rows) if f is None else parts[f]
+        first, n = (0, rows) if f is None else parts[f][:2]
         return pl.ds(pl.multiple_of(j * rows + first, 16), n)
 
+    def load(src, dst, i):
+        return pltpu.make_async_copy(src, dst, in_sem.at[i])
+
+    w_loads = [load(lw_hbm.at[pl.ds(p[0], p[1]), :], lw_ref.at[pl.ds(p[0], p[1]), :], f) for f, p in enumerate(parts)]
     loads = [
-        pltpu.make_async_copy(src, dst, in_sem.at[i])
-        for i, (src, dst) in enumerate(
-            ((lw_hbm, lw_ref), (t_hbm, tg.at[a]), (x_hbm, x_ref), (gw_hbm, gw_ref), (mom_hbm, mom_ref))
-        )
+        load(src, dst, n_parts + i)
+        for i, (src, dst) in enumerate(((t_hbm, tg.at[a]), (x_hbm, x_ref), (gw_hbm, gw_ref), (mom_hbm, mom_ref)))
     ]
-    for ld in loads:
+    for ld in w_loads:
         ld.start()
 
     is_guide = a == 1
@@ -104,8 +110,11 @@
         for t in range(1, n_z):
             tell(barrier, me, z_peer(t)[1])
 
-    loads[0].wait()
-    wg[rows_of(y), :] = lw_ref[...].astype(bf16)
+    for ld in loads:
+        ld.start()
+    for f, p in enumerate(parts):
+        w_loads[f].wait()
+        wg[rows_of(y, f), :] = lw_ref[p[0] : p[0] + p[1], :].astype(bf16)
 
     @pl.when(c == 0)
     def _():
@@ -121,7 +130,12 @@
     def _():
         pl.semaphore_wait(go, 1)
 
-    flows = ((1, 0, half, up, 0), (-1, 1, half, dn, 1), (1, 1, half - 1, up, 0), (-1, 0, half - 1, dn, 1))
+    flows = [
+        (sign, f, hops, up if sign == 1 else dn, int(sign != 1))
+        for far_way, hops in ((1, half), (-1, half - 1))
+        for f, sign in enumerate(far_way * p[2] for p in parts)
+    ]
+    long_flows, short_flows = flows[:n_parts], flows[n_parts:]
 
     def w_copy(o, f, to, d):
         blk = wg.at[rows_of(o, f), :]
@@ -133,7 +147,7 @@
     def gather_step(s):
         for sign, f, hops, to, d in flows:
             if s <= hops:
-                cp = w_copy(wrap(y - sign * s), f, to, d)
+                cp = w_copy(wrap(y - turn * sign * s), f, to, d)
                 cp.wait_recv()
                 if s + 1 <= hops:
                     cp.start()
@@ -145,10 +159,10 @@
         t_copy(a, 0, across).start()
         t_copy(a, 1, mate).start()
 
+    loads[0].wait()
+    pl.when(c == 1)(t_send)
+
     loads[1].wait()
-    pl.when(c == 1)(t_send)
-
-    loads[2].wait()
     tile = 128
     total = jnp.zeros((1, tok), f32)
     for i in range(width // tile):
@@ -172,8 +186,8 @@
     def n_copy(k, to):
         return copy(nown.at[k], nT.at[a], n_snd.at[k], n_rcv.at[a], to)
 
+    loads[2].wait()
     loads[3].wait()
-    loads[4].wait()
     picked = jnp.full((rows, 128), lax.rem(frag_ref[0], hidden // 128), jnp.int32)
     frag_local = lw_ref[:, :128]
     for k in range(1, hidden // 128):
@@ -281,8 +295,8 @@
         return copy(rsout.at[r, :], buf.at[r, :], rs_snd.at[o, f], sem.at[o, f], to)
 
     def reduce_part(s, sign, f):
-        hops = half if (sign == 1) == (f == 0) else half - 1
-        o = wrap(y - sign * s)
+        hops = half if sign == parts[f][2] else half - 1
+        o = wrap(y - turn * sign * s)
         r = rows_of(o, f)
         cp = rs_copy(o, f, sign)
         if s < hops:
@@ -310,10 +324,11 @@
         copy(nown.at[k], nT.at[k], n_snd.at[k], n_rcv.at[k], to).wait_recv()
     far = wrap(y + half)
     g_block(far)
-    reduce_part(4, 1, 0)
-    reduce_part(4, -1, 1)
-    for sign, f in ((1, 1), (-1, 0)):
-        g_block(wrap(y - sign * 3))
+    for sign, f, *_ in long_flows:
+        reduce_part(half, sign, f)
+    for s in (3, -3):
+        g_block(wrap(y + s))
+    for sign, f, *_ in short_flows:
         reduce_part(3, sign, f)
     d_block(wrap(y + 3))
     d_block(wrap(y - 3))
@@ -329,10 +344,10 @@
     din[a] = dout[a]
     for s in (-2, 2, -1, 1, 0):
         g_block(wrap(y + s))
-    for sign, f in ((1, 0), (-1, 1)):
+    for sign, f, *_ in long_flows:
         reduce_part(3, sign, f)
     for s in (2, 1):
-        for sign, f in ((1, 1), (-1, 0), (1, 0), (-1, 1)):
+        for sign, f, *_ in short_flows + long_flows:
             reduce_part(s, sign, f)
         if s == 2:
             rep_end()
@@ -354,7 +369,8 @@
     for i in range(width // tile):
         ig_ref[:, i * tile : (i + 1) * tile] = igT[i * tile : (i + 1) * tile, :].T
 
-    outs = ((ig_ref, ig_out), (nm_ref, nm_out), (ng_ref, ng_out), (nl_ref, nl_out))
+    outs = [(ig_ref, ig_out), (nm_ref, nm_out), (ng_ref, ng_out)]
+    outs += [(nl_ref.at[pl.ds(p[0], p[1]), :], nl_out.at[pl.ds(p[0], p[1]), :]) for p in parts]
     stores = [pltpu.make_async_copy(src, dst, out_sem.at[i]) for i, (src, dst) in enumerate(outs)]
     stores[0].start()
 
@@ -369,9 +385,9 @@
     stores[1].start()
     stores[2].start()
 
-    for f in (1, 0):
+    for f in range(n_parts):
         r = rows_of(y, f)
-        own = slice(parts[f][0], sum(parts[f]))
+        own = slice(parts[f][0], parts[f][0] + parts[f][1])
         for sign in (1, -1):
             rs_copy(y, f, sign).wait_recv()
         for k in range(hidden // 128):
@@ -380,15 +396,14 @@
             inner = lw_ref[own, cols] - (inner_rate * grad) * (1.0 / math.sqrt(tokens_all))
             blended = blend_keep * inner + (1.0 - blend_keep) * ng_ref[own, :]
             nl_ref[own, cols] = jnp.where(picked[own] == k, blended, inner)
-
-    stores[3].start()
+        stores[3 + f].start()
 
     for s in range(half):
         for sign, f, hops, to, d in flows:
             if s + 1 <= hops:
-                w_copy(wrap(y - sign * s), f, to, d).wait_send()
+                w_copy(wrap(y - turn * sign * s), f, to, d).wait_send()
     for s in range(1, n_y):
-        for f in (0, 1):
+        for f in range(n_parts):
             rs_copy(wrap(y + s), f, 1).wait_send()
     for i in range(3):
         t_copy(a, i, mate).wait_send()
@@ -413,12 +428,17 @@
 
 
 def finish(nl_in, ig_in, nm_in, ng_in, nl_out, ig_out, nm_out, ng_out, nl_ref, ig_ref, nm_ref, ng_ref, in_sem, out_sem):
-    def moves(pairs, sem):
-        return [pltpu.make_async_copy(src, dst, sem.at[i]) for i, (src, dst) in enumerate(pairs)]
-
-    held = (ig_ref, nl_ref, nm_ref, ng_ref)
-    loads = moves(zip((ig_in, nl_in, nm_in, ng_in), held), in_sem)
-    stores = moves(zip(held, (ig_out, nl_out, nm_out, ng_out)), out_sem)
+    loads, stores = [], []
+    for src, held, dst, n in (
+        (ig_in, ig_ref, ig_out, 4), (nl_in, nl_ref, nl_out, 3), (nm_in, nm_ref, nm_out, 1), (ng_in, ng_ref, ng_out, 1)
+    ):
+        n = min(n, src.shape[0] // 16)
+        size = src.shape[0] // n // 16 * 16
+        for i in range(n):
+            part = pl.ds(i * size, size if i < n - 1 else src.shape[0] - i * size)
+            at = len(loads)
+            loads.append(pltpu.make_async_copy(src.at[part, :], held.at[part, :], in_sem.at[at]))
+            stores.append(pltpu.make_async_copy(held.at[part, :], dst.at[part, :], out_sem.at[at]))
     for ld in loads:
         ld.start()
     for ld, st in zip(loads, stores):
@@ -440,13 +460,14 @@
         small = global_weights.shape
         n_z = n_rep // 2
         limit = 63 * 1024 * 1024
+        n_parts = min(2, rows // 16)
         smem = pl.BlockSpec(memory_space=pltpu.SMEM)
         hbm = pl.BlockSpec(memory_space=pltpu.HBM)
         dma = pltpu.SemaphoreType.DMA
         V = pltpu.VMEM
         shape = jax.ShapeDtypeStruct
         outs = pl.pallas_call(
-            functools.partial(kernel, n_rep, n_y, tok * n_fsdp),
+            functools.partial(kernel, n_rep, n_y, tok * n_fsdp, n_parts),
             out_shape=(shape((rows, hidden), f32), shape((tok, width), bf16), shape(small, f32), shape(small, f32)),
             in_specs=[smem] + [hbm] * 5,
             out_specs=(hbm,) * 4,
@@ -477,12 +498,12 @@
                 V((n_z, 4 * rows // n_z, small[1]), f32),
                 V((2, 4 * rows // n_z, small[1]), f32),
                 V((4 * rows, small[1]), f32),
-                dma((5,)), dma((4,)),
-                dma((2, n_y, 2)), dma((n_y, 2)),
+                dma((4 + n_parts,)), dma((3 + n_parts,)),
+                dma((2, n_y, n_parts)), dma((n_y, n_parts)),
                 dma((3,)), dma((4,)),
                 dma((4,)), dma((4,)),
                 dma((4,)), dma((4,)),
-                dma((n_y, 2)), dma((n_y, 2)), dma((n_y, 2)),
+                dma((n_y, n_parts)), dma((n_y, n_parts)), dma((n_y, n_parts)),
                 pltpu.SemaphoreType.REGULAR,
                 dma(()), dma((4,)), dma((4,)), dma(()),
                 dma((n_z,)), dma((n_z,)), dma(()), dma(()), dma((n_z,)), dma((n_z,)),
@@ -497,7 +518,7 @@
             in_specs=[hbm] * 4,
             out_specs=(hbm,) * 4,
             scratch_shapes=[
-                V((rows, hidden), f32), V((tok, width), bf16), V(small, f32), V(small, f32), dma((4,)), dma((4,))
+                V((rows, hidden), f32), V((tok, width), bf16), V(small, f32), V(small, f32), dma((9,)), dma((9,))
             ],
             compiler_params=pltpu.CompilerParams(vmem_limit_bytes=limit),
         )(*outs)

time: 58.9 us -> 58.7 us (level)
  no operation moved by 1% of the time
where the time goes in v4:
time: 58.7 us; the launch traced here: 58.5 us
  Pallas kernels  57.2 us (97%)
  between operations  1.29 us (2%)
    pallas_call x1, Pallas kernels, shards(): pl.pallas_call(functools.partial(kernel, n_rep, n_y, tok * n_fsdp, n_part...  54.8 us
    pallas_call x1, Pallas kernels, shards(): pl.pallas_call(finish, out_shape=(shape((rows, hidden), f32), shape((tok,...  2.36 us

profile of v4, /device:TPU:1, one launch (start us, length us, event | category | flops | bytes accessed | tf_op | source)
XLA Modules:
  0.0 58.5 jit_solution(13422138572965557655)
XLA Ops:
  1.3 54.8 %shard_map.93 = (f32[144,1024]{1,0:T(8,128)}, bf16[128,4608]{1,0:T(8,128)(2,1)}, f32[144,128]{1,0:T(8,128)}, f32[144,128]{1,0:T(8,128)}) custom-call(s32[1]{0:T(128)S(6)} %copy.10.frag_ref, bf16[128,4608]{1,0:T(8,128)(2,1)} %bitcast.5, bf16[128,1024]{1,0:T(8,128)(2,1)} %bitcast.7, f32[144,1024]{1,0:T(8,128)} %bitcast.6, f32[144,128]{1,0:T(8,128)} %gw_hbm.1, ...), custom_call_target="tpu_custom_call" | custom-call | tf_op jit(solution)/shard_map/pallas_call | solution.py:469
  56.1 2.4 %shard_map.94 = (f32[144,1024]{1,0:T(8,128)}, bf16[128,4608]{1,0:T(8,128)(2,1)}, f32[144,128]{1,0:T(8,128)}, f32[144,128]{1,0:T(8,128)}) custom-call(f32[144,1024]{1,0:T(8,128)} %get-tuple-element.12.nl_in, bf16[128,4608]{1,0:T(8,128)(2,1)} %get-tuple-element.13.ig_in, f32[144,128]{1,0:T(8,128)} %get-tuple-element.14.nm_in, f32[144,128]{1,0:T(8,128)} %get-tuple-element.15.ng_in), custom_call_target="tpu_custom_call" | custom-call | tf_op jit(solution)/shard_map/pallas_call | solution.py:515

commit v5 on v4

--- a/solution.py
+++ b/solution.py
@@ -144,8 +144,8 @@
     for _, f, _, to, d in flows:
         w_copy(y, f, to, d).start()
 
-    def gather_step(s):
-        for sign, f, hops, to, d in flows:
+    def gather_step(s, ways=flows):
+        for sign, f, hops, to, d in ways:
             if s <= hops:
                 cp = w_copy(wrap(y - turn * sign * s), f, to, d)
                 cp.wait_recv()
@@ -185,6 +185,8 @@
 
     def n_copy(k, to):
         return copy(nown.at[k], nT.at[a], n_snd.at[k], n_rcv.at[a], to)
+
+    gather_step(1, long_flows)
 
     loads[2].wait()
     loads[3].wait()
@@ -307,7 +309,7 @@
             rsout[r, :] = G[r, :].astype(bf16)
         cp.start()
 
-    gather_step(1)
+    gather_step(1, short_flows)
     relay = t_copy(a_across, 2, mate)
     relay.wait_recv()
     relay.start()

time: 58.7 us -> 62.1 us (1.058)
  the two profiles are of different devices: /device:TPU:1 before, /device:TPU:3 now
where the time goes in v5:
time: 62.1 us; the launch traced here: 61.9 us
  Pallas kernels  60.6 us (98%)
  between operations  1.29 us (2%)
    pallas_call x1, Pallas kernels, shards(): pl.pallas_call(functools.partial(kernel, n_rep, n_y, tok * n_fsdp, n_part...  58.2 us
    pallas_call x1, Pallas kernels, shards(): pl.pallas_call(finish, out_shape=(shape((rows, hidden), f32), shape((tok,...  2.36 us

profile of v5, /device:TPU:3, one launch (start us, length us, event | category | flops | bytes accessed | tf_op | source)
XLA Modules:
  0.0 61.9 jit_solution(8834150721893625893)
XLA Ops:
  1.3 58.2 %shard_map.93 = (f32[144,1024]{1,0:T(8,128)}, bf16[128,4608]{1,0:T(8,128)(2,1)}, f32[144,128]{1,0:T(8,128)}, f32[144,128]{1,0:T(8,128)}) custom-call(s32[1]{0:T(128)S(6)} %copy.10.frag_ref, bf16[128,4608]{1,0:T(8,128)(2,1)} %bitcast.5, bf16[128,1024]{1,0:T(8,128)(2,1)} %bitcast.7, f32[144,1024]{1,0:T(8,128)} %bitcast.6, f32[144,128]{1,0:T(8,128)} %gw_hbm.1, ...), custom_call_target="tpu_custom_call" | custom-call | tf_op jit(solution)/shard_map/pallas_call | solution.py:471
  59.5 2.4 %shard_map.94 = (f32[144,1024]{1,0:T(8,128)}, bf16[128,4608]{1,0:T(8,128)(2,1)}, f32[144,128]{1,0:T(8,128)}, f32[144,128]{1,0:T(8,128)}) custom-call(f32[144,1024]{1,0:T(8,128)} %get-tuple-element.12.nl_in, bf16[128,4608]{1,0:T(8,128)(2,1)} %get-tuple-element.13.ig_in, f32[144,128]{1,0:T(8,128)} %get-tuple-element.14.nm_in, f32[144,128]{1,0:T(8,128)} %get-tuple-element.15.ng_in), custom_call_target="tpu_custom_call" | custom-call | tf_op jit(solution)/shard_map/pallas_call | solution.py:517
